TPU v7x, 32 devices: a whole 2x2x4 slice. The times are simulated.
32 devices in a mesh: dp: 8 (over z, y), tensor: 4 (over x, core).
Axes of the slice: x: 2, y: 2, z: 4, core: 2. Of those that a mesh axis runs over, the one named last changes fastest.
Arguments:
- layer_input: bfloat16 [10240, 768], P(('dp', 'tensor')), may hold values from -6 to 6
- cotangent: bfloat16 [10240, 768], P(('dp', 'tensor')), may hold values from -6 to 6
- segments: int32 [10240], replicated, may hold values from 0 to 25, as said below
- parents: int32 [26], replicated, may hold values from 0 to 17, as said below
- norm1_gain: bfloat16 [768], P('dp'), may hold values from 0.099609375 to 1.8984375
- w_query: bfloat16 [768, 768], P('dp', 'tensor'), may hold values from -0.21875 to 0.21875
- w_key: bfloat16 [768, 768], P('dp', 'tensor'), may hold values from -0.21875 to 0.21875
- w_value: bfloat16 [768, 768], P('dp', 'tensor'), may hold values from -0.21875 to 0.21875
- w_out: bfloat16 [768, 768], P('tensor', 'dp'), may hold values from -1.75 to 1.75
- norm2_gain: bfloat16 [768], P('dp'), may hold values from 0.099609375 to 1.8984375
- w_up: bfloat16 [768, 3072], P('dp', 'tensor'), may hold values from -0.21875 to 0.21875
- w_down: bfloat16 [3072, 768], P('tensor', 'dp'), may hold values from -0.109375 to 0.109375
Outputs:
- layer_output: bfloat16 [10240, 768], P(('dp', 'tensor'))
- input_grad: bfloat16 [10240, 768], P(('dp', 'tensor'))
- grad_norm1_gain: float32 [768], P('dp')
- grad_query: float32 [768, 768], P('dp', 'tensor')
- grad_key: float32 [768, 768], P('dp', 'tensor')
- grad_value: float32 [768, 768], P('dp', 'tensor')
- grad_out: float32 [768, 768], P('tensor', 'dp')
- grad_norm2_gain: float32 [768], P('dp')
- grad_up: float32 [768, 3072], P('dp', 'tensor')
- grad_down: float32 [3072, 768], P('tensor', 'dp')
Inputs may be any that keep to these rules, and one draw needn't show every extreme that they name: Tree t holds bytes 5120 t to 5120 (t + 1) - 1 of the stream (the last tree may end at 10240). Its first 2048 bytes are segment 13 t, the trunk; the rest are twelve runs of 256 bytes with the segments 13 t + 1 to 13 t + 12 in some order, every run after the run of its parent segment. parents[s] is the parent segment of s: the trunk 13 t is its own parent, the branches 13 t + 1 to 13 t + 4 have the trunk, and the leaves 13 t + 5 to 13 t + 12 have one of the four branches each, two leaves a branch.
All inputs are finite; a program needn't handle non-finite values.
Results may differ from a plain program's by a relative error of at most 0.017.
Values may be sent and summed in bfloat16 or wider, within the bound.
A program may use at most 256 MiB of HBM per device.

v0:
```python
import math
import jax
import jax.numpy as jnp
from jax import lax
from jax.sharding import PartitionSpec as P

HD = 64
WINDOW = 1536
epsilon = 1e-06
masked_score = -1e30


def from_behind(block, axis, distance):
    devices = range(lax.axis_size(axis))
    route = [(i - distance, i) for i in devices if i - distance in devices]
    return lax.ppermute(block, axis, route)


def split_up(x, dim, peers):
    dims = x.shape
    tiles = x.reshape(*dims[:dim], peers, dims[dim] // peers, *dims[dim + 1 :])
    return jnp.moveaxis(tiles, dim, 0)


def sum_at_owner(x, axis, dim):
    tiles = split_up(x, dim, lax.axis_size(axis))
    arrived = lax.all_to_all(tiles, axis, split_axis=0, concat_axis=0, tiled=True)
    return arrived.astype(jnp.float32).sum(axis=0)


def side_by_side(arrays, axis, dim, along):
    widths = [math.prod(a.shape[along:]) for a in arrays]
    both = jnp.concatenate(
        [a.reshape(*a.shape[:along], w) for a, w in zip(arrays, widths)], axis=along
    )
    whole = sum_at_owner(both, axis, dim)
    tiles = jnp.split(whole, [sum(widths[:k]) for k in range(1, len(widths))], axis=along)
    return tuple((b.reshape(*whole.shape[:along], *a.shape[along:]) for a, b in zip(arrays, tiles)))


def gelu_exact(values):
    return jax.nn.gelu(values, approximate=False)


def row_scale(values):
    return lax.rsqrt(jnp.mean(values * values, axis=-1, keepdims=True) + epsilon)


def norm_backward(incoming, normal_hat, row_factor, gain):
    scaled = incoming * gain
    inner = jnp.mean(scaled * normal_hat, axis=-1, keepdims=True)
    return (row_factor * (scaled - normal_hat * inner), jnp.sum(incoming * normal_hat, axis=0))


def parent_of(seg_ids, parents):
    seg_table = jnp.arange(parents.shape[0], dtype=jnp.int32)
    hits = seg_ids[:, None] == seg_table[None, :]
    return jnp.sum(jnp.where(hits, parents[None, :], 0), axis=1)


def shards(
    layer_input,
    cotangent,
    segments,
    parents,
    norm1_gain,
    w_query,
    w_key,
    w_value,
    w_out,
    norm2_gain,
    w_up,
    w_down,
):
    gain_one, full_query, full_key, full_value, full_out, gain_two, full_up, full_down = (
        lax.all_gather(norm1_gain, "dp", axis=0, tiled=True),
        lax.all_gather(w_query, "dp", axis=0, tiled=True),
        lax.all_gather(w_key, "dp", axis=0, tiled=True),
        lax.all_gather(w_value, "dp", axis=0, tiled=True),
        lax.all_gather(w_out, "dp", axis=1, tiled=True),
        lax.all_gather(norm2_gain, "dp", axis=0, tiled=True),
        lax.all_gather(w_up, "dp", axis=0, tiled=True),
        lax.all_gather(w_down, "dp", axis=1, tiled=True),
    )
    gain_one = gain_one.astype(jnp.float32)
    gain_two = gain_two.astype(jnp.float32)
    row_count = layer_input.shape[0]
    token_count = row_count * lax.axis_size("tensor")
    position = lax.axis_index("dp") * token_count
    head_width = full_query.shape[1]
    head_count = head_width // HD
    scaling = HD ** (-0.5)
    block_rows = min(640, token_count)
    block_count = token_count // block_rows
    span = WINDOW + block_rows
    hop_count = (WINDOW + token_count - 1) // token_count
    inputs = layer_input.astype(jnp.float32)
    factor_one = row_scale(inputs)
    hat_one = inputs * factor_one
    normed = (hat_one * gain_one).astype(jnp.bfloat16)
    normed_all = lax.all_gather(normed, "tensor", axis=0, tiled=True)
    queries = jnp.dot(normed_all, full_query, preferred_element_type=jnp.float32).astype(
        jnp.bfloat16
    )
    keys_own = jnp.dot(normed_all, full_key, preferred_element_type=jnp.float32).astype(
        jnp.bfloat16
    )
    values_own = jnp.dot(normed_all, full_value, preferred_element_type=jnp.float32).astype(
        jnp.bfloat16
    )
    pair_own = jnp.concatenate([keys_own, values_own], axis=1)
    halo_parts = []
    for distance in range(1, hop_count + 1):
        length = min(token_count, WINDOW - (distance - 1) * token_count)
        piece = pair_own[token_count - length :]
        moved = from_behind(piece, "dp", distance)
        halo_parts.append(moved)
    pair_all = jnp.concatenate(halo_parts[::-1] + [pair_own], axis=0)
    seg_padded = jnp.concatenate([jnp.full((WINDOW,), -1, jnp.int32), segments])
    seg_keys = lax.dynamic_slice_in_dim(seg_padded, position, WINDOW + token_count, 0)
    seg_query = seg_keys[WINDOW:]
    parent_one = parent_of(seg_query, parents)
    parent_two = parent_of(parent_one, parents)
    query_spots = jnp.arange(block_rows, dtype=jnp.int32)
    key_spots = jnp.arange(span, dtype=jnp.int32)

    def scores_of(offset):
        query_block = lax.dynamic_slice_in_dim(queries, offset, block_rows, 0).reshape(
            block_rows, head_count, HD
        )
        pair_block = lax.dynamic_slice_in_dim(pair_all, offset, span, 0)
        key_block = pair_block[:, :head_width].reshape(span, head_count, HD)
        value_block = pair_block[:, head_width:].reshape(span, head_count, HD)
        own_seg = lax.dynamic_slice_in_dim(seg_query, offset, block_rows, 0)
        up_one = lax.dynamic_slice_in_dim(parent_one, offset, block_rows, 0)
        up_two = lax.dynamic_slice_in_dim(parent_two, offset, block_rows, 0)
        near_seg = lax.dynamic_slice_in_dim(seg_keys, offset, span, 0)
        gap = WINDOW + query_spots[:, None] - key_spots[None, :]
        same_path = (
            (near_seg[None, :] == own_seg[:, None])
            | (near_seg[None, :] == up_one[:, None])
            | (near_seg[None, :] == up_two[:, None])
        )
        allowed = (gap >= 0) & (gap < WINDOW) & same_path
        raw = (
            jnp.einsum("qhd,khd->hqk", query_block, key_block, preferred_element_type=jnp.float32)
            * scaling
        )
        return (jnp.where(allowed[None], raw, masked_score), query_block, key_block, value_block)

    def forward_block(block_index):
        scores, query_block, key_block, value_block = scores_of(block_index * block_rows)
        row_max = jnp.max(scores, axis=-1, keepdims=True)
        exponent = jnp.exp(scores - row_max)
        denominator = jnp.sum(exponent, axis=-1, keepdims=True)
        weights = (exponent / denominator).astype(jnp.bfloat16)
        mixed = jnp.einsum("hqk,khd->qhd", weights, value_block, preferred_element_type=jnp.float32)
        return (
            mixed.reshape(block_rows, head_width).astype(jnp.bfloat16),
            (row_max + jnp.log(denominator))[..., 0],
        )

    context_blocks, logsum_blocks = lax.map(forward_block, jnp.arange(block_count, dtype=jnp.int32))
    context = context_blocks.reshape(token_count, head_width)
    middle = inputs + lax.psum_scatter(
        jnp.dot(context, full_out, preferred_element_type=jnp.float32).astype(jnp.bfloat16),
        "tensor",
        scatter_dimension=0,
        tiled=True,
    ).astype(jnp.float32)
    factor_two = row_scale(middle)
    hat_two = middle * factor_two
    normed_two = (hat_two * gain_two).astype(jnp.bfloat16)
    normed_two_all = lax.all_gather(normed_two, "tensor", axis=0, tiled=True)
    upper = jnp.dot(normed_two_all, full_up, preferred_element_type=jnp.float32)
    active = gelu_exact(upper).astype(jnp.bfloat16)
    result = middle + lax.psum_scatter(
        jnp.dot(active, full_down, preferred_element_type=jnp.float32).astype(jnp.bfloat16),
        "tensor",
        scatter_dimension=0,
        tiled=True,
    ).astype(jnp.float32)
    incoming = cotangent.astype(jnp.float32)
    incoming_all = lax.all_gather(cotangent, "tensor", axis=0, tiled=True)
    grad_down = jnp.einsum("tf,td->fd", active, incoming_all, preferred_element_type=jnp.float32)
    grad_active = jnp.einsum(
        "td,fd->tf", incoming_all, full_down, preferred_element_type=jnp.float32
    )
    unused_value, gelu_pull = jax.vjp(gelu_exact, upper)
    grad_upper = gelu_pull(grad_active)[0].astype(jnp.bfloat16)
    grad_up = jnp.einsum(
        "tc,tf->cf", normed_two_all, grad_upper, preferred_element_type=jnp.float32
    )
    grad_normed_two = lax.psum_scatter(
        jnp.einsum("tf,cf->tc", grad_upper, full_up, preferred_element_type=jnp.float32).astype(
            jnp.bfloat16
        ),
        "tensor",
        scatter_dimension=0,
        tiled=True,
    ).astype(jnp.float32)
    through_two, gain_two_part = norm_backward(grad_normed_two, hat_two, factor_two, gain_two)
    grad_middle = incoming + through_two
    grad_middle_all = lax.all_gather(grad_middle.astype(jnp.bfloat16), "tensor", axis=0, tiled=True)
    grad_out = jnp.einsum("tc,td->cd", context, grad_middle_all, preferred_element_type=jnp.float32)
    grad_context = jnp.einsum(
        "td,cd->tc", grad_middle_all, full_out, preferred_element_type=jnp.float32
    ).astype(jnp.bfloat16)

    def backward_block(block_index, carry):
        grad_queries, grad_pairs = carry
        offset = block_index * block_rows
        scores, query_block, key_block, value_block = scores_of(offset)
        logsum = lax.dynamic_index_in_dim(logsum_blocks, block_index, 0, keepdims=False)
        probs = jnp.exp(scores - logsum[..., None])
        grad_rows = lax.dynamic_slice_in_dim(grad_context, offset, block_rows, 0).reshape(
            block_rows, head_count, HD
        )
        grad_probs = jnp.einsum(
            "qhd,khd->hqk", grad_rows, value_block, preferred_element_type=jnp.float32
        )
        inner = jnp.sum(probs * grad_probs, axis=-1, keepdims=True)
        grad_scores = (probs * (grad_probs - inner)).astype(jnp.bfloat16)
        grad_query_block = (
            jnp.einsum("hqk,khd->qhd", grad_scores, key_block, preferred_element_type=jnp.float32)
            * scaling
        )
        grad_key_block = (
            jnp.einsum("hqk,qhd->khd", grad_scores, query_block, preferred_element_type=jnp.float32)
            * scaling
        )
        grad_value_block = jnp.einsum(
            "hqk,qhd->khd",
            probs.astype(jnp.bfloat16),
            grad_rows,
            preferred_element_type=jnp.float32,
        )
        grad_queries = lax.dynamic_update_slice_in_dim(
            grad_queries, grad_query_block.reshape(block_rows, head_width), offset, 0
        )
        update = jnp.concatenate(
            [grad_key_block.reshape(span, head_width), grad_value_block.reshape(span, head_width)],
            axis=1,
        )
        current = lax.dynamic_slice_in_dim(grad_pairs, offset, span, 0)
        grad_pairs = lax.dynamic_update_slice_in_dim(grad_pairs, current + update, offset, 0)
        return (grad_queries, grad_pairs)

    start_carry = (
        jnp.zeros((token_count, head_width), jnp.float32),
        jnp.zeros((WINDOW + token_count, 2 * head_width), jnp.float32),
    )
    grad_queries, grad_pairs = lax.fori_loop(0, block_count, backward_block, start_carry)
    grad_own = grad_pairs[WINDOW:]
    for distance in range(1, hop_count + 1):
        length = min(token_count, WINDOW - (distance - 1) * token_count)
        first_row = WINDOW - (distance - 1) * token_count - length
        piece = grad_pairs[first_row : first_row + length]
        returned = from_behind(piece.astype(jnp.bfloat16), "dp", -distance).astype(piece.dtype)
        grad_own = grad_own + jnp.pad(returned, ((token_count - length, 0), (0, 0)))
    grad_keys = grad_own[:, :head_width].astype(jnp.bfloat16)
    grad_values = grad_own[:, head_width:].astype(jnp.bfloat16)
    grad_queries_low = grad_queries.astype(jnp.bfloat16)
    grad_query = jnp.einsum(
        "tc,tq->cq", normed_all, grad_queries_low, preferred_element_type=jnp.float32
    )
    grad_key = jnp.einsum("tc,tq->cq", normed_all, grad_keys, preferred_element_type=jnp.float32)
    grad_value = jnp.einsum(
        "tc,tq->cq", normed_all, grad_values, preferred_element_type=jnp.float32
    )
    part_query = jnp.einsum(
        "tq,cq->tc", grad_queries_low, full_query, preferred_element_type=jnp.float32
    )
    part_key = jnp.einsum("tq,cq->tc", grad_keys, full_key, preferred_element_type=jnp.float32)
    part_value = jnp.einsum(
        "tq,cq->tc", grad_values, full_value, preferred_element_type=jnp.float32
    )
    grad_normed = lax.psum_scatter(
        (part_query + part_key + part_value).astype(jnp.bfloat16),
        "tensor",
        scatter_dimension=0,
        tiled=True,
    ).astype(jnp.float32)
    through_one, gain_one_part = norm_backward(grad_normed, hat_one, factor_one, gain_one)
    grad_inputs = grad_middle + through_one
    gain_one_sum, gain_two_sum = lax.psum((gain_one_part, gain_two_part), "tensor")
    summed = (
        *side_by_side(
            (
                gain_one_sum.astype(jnp.bfloat16),
                grad_query.astype(jnp.bfloat16),
                grad_key.astype(jnp.bfloat16),
                grad_value.astype(jnp.bfloat16),
            ),
            "dp",
            0,
            1,
        ),
        sum_at_owner(grad_out.astype(jnp.bfloat16), "dp", 1),
        *side_by_side(
            (gain_two_sum.astype(jnp.bfloat16), grad_up.astype(jnp.bfloat16)), "dp", 0, 1
        ),
        sum_at_owner(grad_down.astype(jnp.bfloat16), "dp", 1),
    )
    return (
        result.astype(jnp.bfloat16),
        grad_inputs.astype(jnp.bfloat16),
        summed[0],
        summed[1],
        summed[2],
        summed[3],
        summed[4],
        summed[5],
        summed[6],
        summed[7],
    )


def solution(mesh):
    return jax.shard_map(
        shards,
        mesh=mesh,
        in_specs=(
            P(("dp", "tensor"), None),
            P(("dp", "tensor"), None),
            P(),
            P(),
            P("dp"),
            P("dp", "tensor"),
            P("dp", "tensor"),
            P("dp", "tensor"),
            P("tensor", "dp"),
            P("dp"),
            P("dp", "tensor"),
            P("tensor", "dp"),
        ),
        out_specs=(
            P(("dp", "tensor"), None),
            P(("dp", "tensor"), None),
            P("dp"),
            P("dp", "tensor"),
            P("dp", "tensor"),
            P("dp", "tensor"),
            P("tensor", "dp"),
            P("dp"),
            P("dp", "tensor"),
            P("tensor", "dp"),
        ),
        check_vma=False,
    )
```

profile of v0, /device:TPU:0, one launch (start us, length us, event | category | flops | bytes accessed | tf_op | source)
XLA Modules:
  0.0 772.6 jit_solution(16327131825716059331)
XLA Ops:
  12.9 23.7 %all-reduce.5 = (bf16[768]{0:T(1024)(128)(2,1)S(1)}, bf16[768]{0:T(1024)(128)(2,1)}) all-reduce(bf16[768]{0:T(1024)(128)(2,1)S(1)} %dynamic-update-slice, bf16[768]{0:T(1024)(128)(2,1)S(1)} %dynamic-update-slice.1), channel_id=1, replica_groups=mesh['dp'=8,'tensor'=4] {'dp'}, use_global_device_ids=true, to_apply=%add.2 | all-reduce | flops 1536 | bytes 6144
  41.0 31.2 %all_gather.38 = bf16[768,192]{1,0:T(8,128)(2,1)S(1)} all-gather(bf16[96,192]{1,0:T(8,128)(2,1)} %param.22), channel_id=1, replica_groups=mesh['dp'=8,'tensor'=4] {'dp'}, dimensions={0}, use_global_device_ids=true | all-gather | bytes 331776 | tf_op jit(solution)/shard_map/all_gather | solution.py:78
  72.2 31.2 %all_gather.39 = bf16[768,192]{1,0:T(8,128)(2,1)S(1)} all-gather(bf16[96,192]{1,0:T(8,128)(2,1)} %param.23), channel_id=1, replica_groups=mesh['dp'=8,'tensor'=4] {'dp'}, dimensions={0}, use_global_device_ids=true | all-gather | bytes 331776 | tf_op jit(solution)/shard_map/all_gather | solution.py:79
  110.2 46.0 %all_gather.41 = bf16[192,768]{0,1:T(8,128)(2,1)} all-gather(bf16[192,96]{0,1:T(8,128)(2,1)S(1)} %copy.48), channel_id=1, replica_groups=mesh['dp'=8,'tensor'=4] {'dp'}, dimensions={1}, use_global_device_ids=true | all-gather | bytes 331776 | tf_op jit(solution)/shard_map/all_gather | solution.py:80
  156.2 31.0 %all_gather.40 = bf16[768,192]{1,0:T(8,128)(2,1)S(1)} all-gather(bf16[96,192]{1,0:T(8,128)(2,1)S(1)} %copy-done.35), channel_id=1, replica_groups=mesh['dp'=8,'tensor'=4] {'dp'}, dimensions={0}, use_global_device_ids=true | all-gather | bytes 331776 | tf_op jit(solution)/shard_map/all_gather | solution.py:77
  193.2 72.5 %while.29 = (s32[]{:T(128)}, bf16[2,640,192]{1,2,0:T(8,128)(2,1)}, f32[2,3,640]{2,1,0:T(4,128)S(1)}, s32[2]{0:T(128)S(1)}, bf16[2816,384]{0,1:T(8,128)(2,1)}, /*...) while((s32[]{:T(128)}, bf16[2,640,192]{1,2,0:T(8,128)(2,1)}, ...), condition=%wide.region_6.7_spmd.clone, body=%wide.region_3.6_spmd.clone.sunk | while | flops 1133730560 | bytes 66249560 | solution.py:163
  201.3 8.0 %fusion.136 = (f32[3,640]{1,0:T(4,128)S(1)}, f32[3,640,2176]{2,1,0:T(8,128)}) fusion(pred[640,2176]{1,0:T(8,128)(4,1)S(1)} %fusion.135, bf16[640,3,64]{0,2,1:T(8,128)(2,1)S(1)} %bitcast.146, bf16[2176,3,64]{0,2,1:T(8,128)(2,1)S(1)} %bitcast.145), kind=kOutput, calls=%fused_computation.7.clone.1 | convolution fusion | flops 547305600 | bytes 19193344 | tf_op jit(solution)/shard_map/while/body/eval_jaxpr/qhd,khd->hqk/dot_general | solution.py:146
  209.3 10.5 %fusion.137 = f32[3,640]{1,0:T(4,128)S(1)} fusion(f32[3,640,2176]{2,1,0:T(8,128)} %get-tuple-element.566, f32[3,640]{1,0:T(4,128)S(1)} %get-tuple-element.567, pred[640,2176]{1,0:T(8,128)(4,1)S(1)} %fusion.135), kind=kLoop, calls=%fused_computation.8.clone.1 | loop fusion | flops 16709760 | bytes 18119680 | tf_op jit(solution)/shard_map/while/body/eval_jaxpr/reduce_sum | solution.py:155
  219.8 8.8 %fusion.138 = bf16[3,64,640]{2,1,0:T(8,128)(2,1)S(1)} fusion(bf16[2176,3,64]{0,2,1:T(8,128)(2,1)S(1)} %bitcast.144, f32[3,640,2176]{2,1,0:T(8,128)} %get-tuple-element.566, f32[3,640]{1,0:T(4,128)S(1)} %fusion.137, f32[3,640]{1,0:T(4,128)S(1)} %get-tuple-element.567, pred[640,2176]{1,0:T(8,128)(4,1)S(1)} %fusion.135), kind=kOutput, calls=%fused_computation.15.clone.1 | convolution fusion | flops 555786240 | bytes 19201024 | tf_op jit(solution)/shard_map/while/body/eval_jaxpr/hqk,khd->qhd/dot_general | solution.py:157
  237.5 8.0 %fusion.136 = (f32[3,640]{1,0:T(4,128)S(1)}, f32[3,640,2176]{2,1,0:T(8,128)}) fusion(pred[640,2176]{1,0:T(8,128)(4,1)S(1)} %fusion.135, bf16[640,3,64]{0,2,1:T(8,128)(2,1)S(1)} %bitcast.146, bf16[2176,3,64]{0,2,1:T(8,128)(2,1)S(1)} %bitcast.145), kind=kOutput, calls=%fused_computation.7.clone.1 | convolution fusion | flops 547305600 | bytes 19193344 | tf_op jit(solution)/shard_map/while/body/eval_jaxpr/qhd,khd->hqk/dot_general | solution.py:146
  245.5 10.5 %fusion.137 = f32[3,640]{1,0:T(4,128)S(1)} fusion(f32[3,640,2176]{2,1,0:T(8,128)} %get-tuple-element.566, f32[3,640]{1,0:T(4,128)S(1)} %get-tuple-element.567, pred[640,2176]{1,0:T(8,128)(4,1)S(1)} %fusion.135), kind=kLoop, calls=%fused_computation.8.clone.1 | loop fusion | flops 16709760 | bytes 18119680 | tf_op jit(solution)/shard_map/while/body/eval_jaxpr/reduce_sum | solution.py:155
  256.0 8.9 %fusion.138 = bf16[3,64,640]{2,1,0:T(8,128)(2,1)S(1)} fusion(bf16[2176,3,64]{0,2,1:T(8,128)(2,1)S(1)} %bitcast.144, f32[3,640,2176]{2,1,0:T(8,128)} %get-tuple-element.566, f32[3,640]{1,0:T(4,128)S(1)} %fusion.137, f32[3,640]{1,0:T(4,128)S(1)} %get-tuple-element.567, pred[640,2176]{1,0:T(8,128)(4,1)S(1)} %fusion.135), kind=kOutput, calls=%fused_computation.15.clone.1 | convolution fusion | flops 555786240 | bytes 19201024 | tf_op jit(solution)/shard_map/while/body/eval_jaxpr/hqk,khd->qhd/dot_general | solution.py:157
  271.0 32.7 %reduce-scatter.5.cloned.1.call-done = bf16[320,768]{1,0:T(8,128)(2,1)} async-done(((bf16[1280,768]{1,0:T(8,128)(2,1)}), bf16[320,768]{1,0:T(8,128)(2,1)}) %reduce-scatter.5.cloned.1.call-update) | async-done | bytes 491536 | tf_op jit(solution)/shard_map/reduce_scatter | solution.py:165
  308.4 8.9 %all-gather.11.cloned.1.call-done = bf16[768,768]{1,0:T(8,128)(2,1)} async-done(((bf16[96,768]{1,0:T(8,128)(2,1)}), bf16[768,768]{1,0:T(8,128)(2,1)}) %all-gather.11.cloned.1.call-update) | async-done | bytes 1179664 | tf_op jit(solution)/shard_map/all_gather | solution.py:82
  317.4 22.3 %all-gather.9.cloned.1.call-done = bf16[1280,768]{1,0:T(8,128)(2,1)} async-done(((bf16[320,768]{1,0:T(8,128)(2,1)}), bf16[1280,768]{1,0:T(8,128)(2,1)}) %all-gather.9.cloned.1.call-update) | async-done | bytes 1966096 | tf_op jit(solution)/shard_map/all_gather | solution.py:174
  345.1 38.4 %all-gather.13.cloned.1.call-done = bf16[768,768]{0,1:T(8,128)(2,1)} async-done(((bf16[768,96]{0,1:T(8,128)(2,1)}), bf16[768,768]{0,1:T(8,128)(2,1)}) %all-gather.13.cloned.1.call-update) | async-done | bytes 1179664 | tf_op jit(solution)/shard_map/all_gather | solution.py:83
  383.5 21.9 %all-gather.15.cloned.1.call-done = bf16[1280,768]{1,0:T(8,128)(2,1)} async-done(((bf16[320,768]{1,0:T(8,128)(2,1)}), bf16[1280,768]{1,0:T(8,128)(2,1)}) %all-gather.15.cloned.1.call-update) | async-done | bytes 1966096 | tf_op jit(solution)/shard_map/all_gather | solution.py:184
  405.4 13.1 %add_convert_fusion = (bf16[1280,768]{1,0:T(8,128)(2,1)S(1)}, f32[1280,768]{1,0:T(8,128)}) fusion(f32[1280,768]{1,0:T(8,128)} %fusion.64, bf16[1280,768]{1,0:T(8,128)(2,1)} %all-gather.15.cloned.1.call-done, bf16[768,768]{0,1:T(8,128)(2,1)} %all-gather.13.cloned.1.call-done), kind=kOutput, calls=%fused_computation.47 | convolution fusion | flops 1580728320 | bytes 12976128 | tf_op jit(solution)/shard_map/td,fd->tf/dot_general | solution.py:186
  424.3 30.7 %reduce-scatter.9.cloned.1.call-done = bf16[320,768]{1,0:T(8,128)(2,1)} async-done(((bf16[1280,768]{1,0:T(8,128)(2,1)}), bf16[320,768]{1,0:T(8,128)(2,1)}) %reduce-scatter.9.cloned.1.call-update) | async-done | bytes 491536 | tf_op jit(solution)/shard_map/reduce_scatter | solution.py:194
  459.9 21.4 %all-gather.17.cloned.1.call-done = bf16[1280,768]{1,0:T(8,128)(2,1)} async-done(((bf16[320,768]{1,0:T(8,128)(2,1)}), bf16[1280,768]{1,0:T(8,128)(2,1)}) %all-gather.17.cloned.1.call-update) | async-done | bytes 1966096 | tf_op jit(solution)/shard_map/all_gather | solution.py:204
  487.6 112.6 %while.30 = (s32[]{:T(128)}, bf16[1280,192]{0,1:T(8,128)(2,1)}, f32[2816,384]{0,1:T(8,128)}, bf16[2816,384]{0,1:T(8,128)(2,1)}, s32[2816]{0:T(1024)S(1)}, /*inde...) while((s32[]{:T(128)}, bf16[1280,192]{0,1:T(8,128)(2,1)}, ...), condition=%wide.region_14.15_spmd.clone, body=%wide.region_12.14_spmd.clone.sunk | while | flops 2727729920 | bytes 220916592 | solution.py:253
  495.2 8.1 %fusion.150 = f32[3,640,2176]{2,1,0:T(8,128)} fusion(bf16[640,3,64]{0,2,1:T(8,128)(2,1)S(1)} %bitcast.141, bf16[2176,3,64]{0,2,1:T(8,128)(2,1)S(1)} %bitcast.140), kind=kOutput, calls=%fused_computation.138.clone.1 | convolution fusion | flops 534773760 | bytes 17793024 | tf_op jit(solution)/shard_map/while/body/eval_jaxpr/qhd,khd->hqk/dot_general | solution.py:219
  503.3 15.1 %multiply_reduce_fusion.3 = (f32[3,640]{1,0:T(4,128)S(1)}, f32[3,640,2176]{2,1,0:T(8,128)}) fusion(f32[3,640,2176]{2,1,0:T(8,128)} %fusion.150, f32[3,640]{1,0:T(4,128)S(1)} %dynamic-slice_bitcast_fusion.2, bf16[640,3,64]{0,2,1:T(8,128)(2,1)S(1)} %bitcast.138, bf16[2176,3,64]{0,2,1:T(8,128)(2,1)S(1)} %bitcast.135, pred[640,2176]{1,0:T(8,128)(4,1)S(1)} %fusion.151), kind=kOutput, calls=%fused_computation.24.clone.1 | convolution fusion | flops 555661440 | bytes 35912704 | tf_op jit(solution)/shard_map/while/body/eval_jaxpr/qhd,khd->hqk/dot_general | solution.py:146
  518.5 11.4 %multiply_convert_fusion.4 = bf16[3,640,2176]{2,1,0:T(8,128)(2,1)S(1)} fusion(f32[3,640,2176]{2,1,0:T(8,128)} %get-tuple-element.583, f32[3,640,2176]{2,1,0:T(8,128)} %fusion.150, f32[3,640]{1,0:T(4,128)S(1)} %get-tuple-element.584), kind=kLoop, calls=%fused_computation.23.clone.1 | loop fusion | flops 12533760 | bytes 41786880 | tf_op jit(solution)/shard_map/while/body/eval_jaxpr/convert_element_type | solution.py:223
  551.5 8.1 %fusion.150 = f32[3,640,2176]{2,1,0:T(8,128)} fusion(bf16[640,3,64]{0,2,1:T(8,128)(2,1)S(1)} %bitcast.141, bf16[2176,3,64]{0,2,1:T(8,128)(2,1)S(1)} %bitcast.140), kind=kOutput, calls=%fused_computation.138.clone.1 | convolution fusion | flops 534773760 | bytes 17793024 | tf_op jit(solution)/shard_map/while/body/eval_jaxpr/qhd,khd->hqk/dot_general | solution.py:219
  559.6 15.1 %multiply_reduce_fusion.3 = (f32[3,640]{1,0:T(4,128)S(1)}, f32[3,640,2176]{2,1,0:T(8,128)}) fusion(f32[3,640,2176]{2,1,0:T(8,128)} %fusion.150, f32[3,640]{1,0:T(4,128)S(1)} %dynamic-slice_bitcast_fusion.2, bf16[640,3,64]{0,2,1:T(8,128)(2,1)S(1)} %bitcast.138, bf16[2176,3,64]{0,2,1:T(8,128)(2,1)S(1)} %bitcast.135, pred[640,2176]{1,0:T(8,128)(4,1)S(1)} %fusion.151), kind=kOutput, calls=%fused_computation.24.clone.1 | convolution fusion | flops 555661440 | bytes 35912704 | tf_op jit(solution)/shard_map/while/body/eval_jaxpr/qhd,khd->hqk/dot_general | solution.py:146
  574.7 11.4 %multiply_convert_fusion.4 = bf16[3,640,2176]{2,1,0:T(8,128)(2,1)S(1)} fusion(f32[3,640,2176]{2,1,0:T(8,128)} %get-tuple-element.583, f32[3,640,2176]{2,1,0:T(8,128)} %fusion.150, f32[3,640]{1,0:T(4,128)S(1)} %get-tuple-element.584), kind=kLoop, calls=%fused_computation.23.clone.1 | loop fusion | flops 12533760 | bytes 41786880 | tf_op jit(solution)/shard_map/while/body/eval_jaxpr/convert_element_type | solution.py:223
  606.3 27.3 %collective-permute-done.3 = bf16[256,384]{0,1:T(8,128)(2,1)S(1)} collective-permute-done((bf16[256,384]{0,1:T(8,128)(2,1)S(1)}, bf16[256,384]{0,1:T(8,128)(2,1)S(1)}, u32[]{:S(2)}, u32[]{:S(2)}) %collective-permute-start.3) | collective-permute-done | bytes 196640 | tf_op jit(solution)/shard_map/ppermute | solution.py:16
  667.0 11.4 %all-to-all-done.3 = bf16[8,768,96]{1,2,0:T(8,128)(2,1)} async-done(((bf16[8,768,96]{1,2,0:T(8,128)(2,1)}), bf16[8,768,96]{1,2,0:T(8,128)(2,1)}, u32[]{:S(2)}, u32[]{:S(2)}) %all-to-all-start.3) | async-done | bytes 1179680 | tf_op jit(solution)/shard_map/all_to_all | solution.py:27
  686.5 6.5 all-reduce.4
  710.6 15.5 %all-to-all-done = bf16[8,96,577]{2,1,0:T(8,128)(2,1)S(1)} async-done(((bf16[8,96,577]{2,1,0:T(8,128)(2,1)}), bf16[8,96,577]{2,1,0:T(8,128)(2,1)S(1)}, u32[]{:S(2)}, u32[]{:S(2)}) %all-to-all-start) | async-done | bytes 886304 | tf_op jit(solution)/shard_map/all_to_all | solution.py:27
  739.1 24.3 %all-to-all-done.2 = bf16[8,96,769]{2,1,0:T(8,128)(2,1)S(1)} async-done(((bf16[8,96,769]{2,1,0:T(8,128)(2,1)}), bf16[8,96,769]{2,1,0:T(8,128)(2,1)S(1)}, u32[]{:S(2)}, u32[]{:S(2)}) %all-to-all-start.2) | async-done | bytes 1181216 | tf_op jit(solution)/shard_map/all_to_all | solution.py:27
  (258 shorter events, 192.4 us)
Async XLA Ops:
  8.0 95.4 %all-gather.7.cloned.1.call-start = ((), (), s32[]{:S(2)}) async-start(), calls=%async_computation.8 | async-start | bytes 2457600 | tf_op jit(solution)/shard_map/all_gather | solution.py:101
  9.3 30.9 %copy-start.36 = (f32[320]{0:T(512)}, f32[320]{0:T(512)S(1)}, u32[]{:S(2)}) copy-start(f32[320]{0:T(512)S(1)} %add_rsqrt_fusion.1) | copy-start | bytes 3844
  39.2 264.5 %reduce-scatter.5.cloned.1.call-start = ((), (), s32[]{:S(2)}) async-start(), calls=%async_computation.9 | async-start | bytes 2457600 | tf_op jit(solution)/shard_map/reduce_scatter | solution.py:165
  72.2 36.3 %copy-start.19 = (bf16[768,192]{1,0:T(8,128)(2,1)}, bf16[768,192]{1,0:T(8,128)(2,1)S(1)}, u32[]{:S(2)}) copy-start(bf16[768,192]{1,0:T(8,128)(2,1)S(1)} %all_gather.38) | copy-start | bytes 884740
  103.4 52.9 %copy-start.21 = (bf16[768,192]{1,0:T(8,128)(2,1)}, bf16[768,192]{1,0:T(8,128)(2,1)S(1)}, u32[]{:S(2)}) copy-start(bf16[768,192]{1,0:T(8,128)(2,1)S(1)} %all_gather.39) | copy-start | bytes 884740
  103.4 52.9 %copy-start.35 = (bf16[96,192]{1,0:T(8,128)(2,1)S(1)}, bf16[96,192]{1,0:T(8,128)(2,1)}, u32[]{:S(2)}) copy-start(bf16[96,192]{1,0:T(8,128)(2,1)} %param.21) | copy-start | bytes 110596
  105.9 82.6 %copy-start.3 = (bf16[1280,768]{1,0:T(8,128)(2,1)S(1)}, bf16[1280,768]{1,0:T(8,128)(2,1)}, u32[]{:S(2)}) copy-start(bf16[1280,768]{1,0:T(8,128)(2,1)} %all-gather.7.cloned.1.call-done) | copy-start | bytes 5898244
  108.5 83.2 %collective-permute-start.1 = (bf16[1280,384]{0,1:T(8,128)(2,1)S(1)}, bf16[1280,384]{0,1:T(8,128)(2,1)S(1)}, u32[]{:S(2)}, u32[]{:S(2)}) collective-permute-start(bf16[1280,384]{0,1:T(8,128)(2,1)S(1)} %pad_maximum_fusion.1), channel_id=1, source_target_pairs={{0,4},{4,8},{8,12},{12,16},{16,20},{20,24},{24,28},{1,5},{5,9},{9,... | collective-permute-start | bytes 2949128 | tf_op jit(solution)/shard_map/ppermute | solution.py:16
  187.2 4.5 collective-permute-start
  265.7 38.0 %copy-start.1 = (bf16[320,768]{1,0:T(8,128)(2,1)S(1)}, bf16[320,768]{1,0:T(8,128)(2,1)}, u32[]{:S(2)}) copy-start(bf16[320,768]{1,0:T(8,128)(2,1)} %param.16) | copy-start | bytes 1474564
  266.9 40.2 %copy-start.10 = (bf16[2,24,8,640]{3,2,0,1:T(8,128)(2,1)}, bf16[2,24,8,640]{3,2,0,1:T(8,128)(2,1)S(1)}, u32[]{:S(2)}) copy-start(bf16[2,24,8,640]{3,2,0,1:T(8,128)(2,1)S(1)} %copy.67) | copy-start | bytes 1474564
  270.1 47.3 %all-gather.11.cloned.1.call-start = ((), (), s32[]{:S(2)}) async-start(), calls=%async_computation.11 | async-start | bytes 1327104 | tf_op jit(solution)/shard_map/all_gather | solution.py:82
  270.7 69.0 %all-gather.9.cloned.1.call-start = ((), (), s32[]{:S(2)}) async-start(), calls=%async_computation.10 | async-start | bytes 2457600 | tf_op jit(solution)/shard_map/all_gather | solution.py:174
  271.0 186.2 %copy-start.29 = (f32[768]{0:T(1024)}, f32[768]{0:T(1024)S(1)}, u32[]{:S(2)}) copy-start(f32[768]{0:T(1024)S(1)} %convert_element_type.159) | copy-start | bytes 9220
  305.0 152.2 %copy-start.33 = (f32[320]{0:T(512)}, f32[320]{0:T(512)S(1)}, u32[]{:S(2)}) copy-start(f32[320]{0:T(512)S(1)} %add_rsqrt_fusion) | copy-start | bytes 3844
  307.1 76.4 %all-gather.13.cloned.1.call-start = ((), (), s32[]{:S(2)}) async-start(), calls=%async_computation.12 | async-start | bytes 1327104 | tf_op jit(solution)/shard_map/all_gather | solution.py:83
  307.6 97.7 %all-gather.15.cloned.1.call-start = ((), (), s32[]{:S(2)}) async-start(), calls=%async_computation.14 | async-start | bytes 2457600 | tf_op jit(solution)/shard_map/all_gather | solution.py:184
  308.4 146.7 %reduce-scatter.9.cloned.1.call-start = ((), (), s32[]{:S(2)}) async-start(), calls=%async_computation.15 | async-start | bytes 2457600 | tf_op jit(solution)/shard_map/reduce_scatter | solution.py:194
  419.8 35.2 %copy-start.5 = (bf16[320,768]{1,0:T(8,128)(2,1)S(1)}, bf16[320,768]{1,0:T(8,128)(2,1)}, u32[]{:S(2)}) copy-start(bf16[320,768]{1,0:T(8,128)(2,1)} %reduce-scatter.5.cloned.1.call-done) | copy-start | bytes 1474564
  419.8 37.4 %copy-start.7 = (bf16[320,768]{1,0:T(8,128)(2,1)S(1)}, bf16[320,768]{1,0:T(8,128)(2,1)}, u32[]{:S(2)}) copy-start(bf16[320,768]{1,0:T(8,128)(2,1)} %param.17) | copy-start | bytes 1474564
  424.2 57.0 %copy-start.25 = (bf16[192,768]{0,1:T(8,128)(2,1)S(1)}, bf16[192,768]{0,1:T(8,128)(2,1)}, u32[]{:S(2)}) copy-start(bf16[192,768]{0,1:T(8,128)(2,1)} %all_gather.41) | copy-start | bytes 884740
  424.2 57.0 %all-gather.17.cloned.1.call-start = ((), (), s32[]{:S(2)}) async-start(), calls=%async_computation.16 | async-start | bytes 2457600 | tf_op jit(solution)/shard_map/all_gather | solution.py:204
  457.2 30.4 %copy-start.38 = (f32[320]{0:T(512)}, f32[320]{0:T(512)S(1)}, u32[]{:S(2)}) copy-start(f32[320]{0:T(512)S(1)} %broadcast_multiply_fusion.1) | copy-start | bytes 3844
  459.4 225.5 %reduce-scatter.11.cloned.1.call-start = ((), (), s32[]{:S(2)}) async-start(), calls=%async_computation.17 | async-start | bytes 2457600 | tf_op jit(solution)/shard_map/reduce_scatter | solution.py:278
  602.8 30.9 %collective-permute-start.2 = (bf16[1280,384]{0,1:T(8,128)(2,1)S(1)}, bf16[1280,384]{0,1:T(8,128)(2,1)S(1)}, u32[]{:S(2)}, u32[]{:S(2)}) collective-permute-start(bf16[1280,384]{0,1:T(8,128)(2,1)S(1)} %slice.58), channel_id=1, source_target_pairs={{4,0},{8,4},{12,8},{16,12},{20,16},{24,20},{28,24},{5,1},{9,5},{13... | collective-permute-start | bytes 2949128 | tf_op jit(solution)/shard_map/ppermute | solution.py:16
  604.3 29.4 %collective-permute-start.3 = (bf16[256,384]{0,1:T(8,128)(2,1)S(1)}, bf16[256,384]{0,1:T(8,128)(2,1)S(1)}, u32[]{:S(2)}, u32[]{:S(2)}) collective-permute-start(bf16[256,384]{0,1:T(8,128)(2,1)S(1)} %slice.59), channel_id=1, source_target_pairs={{8,0},{12,4},{16,8},{20,12},{24,16},{28,20},{9,1},{13,5},{17,9},{2... | collective-permute-start | bytes 589832 | tf_op jit(solution)/shard_map/ppermute | solution.py:16
  605.6 29.9 %copy-start.20 = (bf16[768,192]{1,0:T(8,128)(2,1)S(1)}, bf16[768,192]{1,0:T(8,128)(2,1)}, u32[]{:S(2)}) copy-start(bf16[768,192]{1,0:T(8,128)(2,1)} %copy-done.19) | copy-start | bytes 884740
  645.7 32.7 %all-to-all-start.3 = ((bf16[8,768,96]{1,2,0:T(8,128)(2,1)}), bf16[8,768,96]{1,2,0:T(8,128)(2,1)}, u32[]{:S(2)}, u32[]{:S(2)}) async-start(bf16[8,768,96]{1,2,0:T(8,128)(2,1)} %bitcast.154), calls=%async_computation.7 | async-start | bytes 2359296 | tf_op jit(solution)/shard_map/all_to_all | solution.py:27
  650.0 84.5 %reduce-scatter.7.cloned.1.call-start = ((), (), s32[]{:S(2)}) async-start(), calls=%async_computation.13 | async-start | bytes 2457600 | tf_op jit(solution)/shard_map/reduce_scatter | solution.py:177
  678.4 17.6 %all-to-all-start.1 = ((bf16[8,192,96]{2,1,0:T(8,128)(2,1)}), bf16[8,192,96]{2,1,0:T(8,128)(2,1)}, u32[]{:S(2)}, u32[]{:S(2)}) async-start(bf16[8,192,96]{2,1,0:T(8,128)(2,1)} %bitcast.150), calls=%async_computation.5 | async-start | bytes 786432 | tf_op jit(solution)/shard_map/all_to_all | solution.py:27
  696.0 30.0 %all-to-all-start = ((bf16[8,96,577]{2,1,0:T(8,128)(2,1)}), bf16[8,96,577]{2,1,0:T(8,128)(2,1)S(1)}, u32[]{:S(2)}, u32[]{:S(2)}) async-start(bf16[8,96,577]{2,1,0:T(8,128)(2,1)} %pad_maximum_fusion.2), calls=%async_computation.4 | async-start | bytes 1966080 | tf_op jit(solution)/shard_map/all_to_all | solution.py:27
  727.0 36.4 %all-to-all-start.2 = ((bf16[8,96,769]{2,1,0:T(8,128)(2,1)}), bf16[8,96,769]{2,1,0:T(8,128)(2,1)S(1)}, u32[]{:S(2)}, u32[]{:S(2)}) async-start(bf16[8,96,769]{2,1,0:T(8,128)(2,1)} %pad_maximum_fusion), calls=%async_computation.6 | async-start | bytes 2752512 | tf_op jit(solution)/shard_map/all_to_all | solution.py:27
  (36 other events, 395.1 us)
Sparse Core Ops, SparseCore 0:
  39.3 19.0 all-gather.6
  270.2 33.4 reduce-scatter.4
  424.4 30.6 reduce-scatter.8
  639.0 28.7 reduce-scatter.10
  670.4 30.8 reduce-scatter.6
Sparse Core Ops, SparseCore 1:
  273.0 44.3 all-gather.10
  319.5 20.1 all-gather.8
  342.0 41.5 all-gather.12
  385.2 20.1 all-gather.14
  459.5 21.7 all-gather.16
where the time goes:
time: 778 us; the launch traced here: 773 us
  waiting for transfers between devices  259 us (33%)
  blocking collectives  170 us (22%)
  matrix products  150 us (19%)
  other arithmetic  107 us (14%)
  local copies, waits for them, and re-layouts  43.4 us (6%)
  starting transfers between devices  24.5 us (3%)
  between operations  17 us (2%)
    all_to_all x4, waiting for transfers between devices, sum_at_owner(): lax.all_to_all(tiles, axis, split_axis=0, concat_axis=0, tiled=True)  51.2 us
    dot_general x4, matrix products, scores_of(): jnp.einsum('qhd,khd->hqk', query_block, key_block, preferred_element_type...  46.3 us
    all_gather x1, blocking collectives, shards(): lax.all_gather(w_out, 'dp', axis=1, tiled=True)  46 us
    all_gather x1, waiting for transfers between devices, shards(): lax.all_gather(w_down, 'dp', axis=1, tiled=True)  38.4 us
    reduce_scatter x1, waiting for transfers between devices, shards(): lax.psum_scatter(jnp.dot(context, full_out, preferred_element_type=jnp.fl...  32.7 us
    all_gather x1, blocking collectives, shards(): lax.all_gather(w_key, 'dp', axis=0, tiled=True)  31.2 us
    all_gather x1, blocking collectives, shards(): lax.all_gather(w_value, 'dp', axis=0, tiled=True)  31.2 us
    all_gather x1, blocking collectives, shards(): lax.all_gather(w_query, 'dp', axis=0, tiled=True)  31 us
  transfers between devices with their start and end apart: 18, of which 12 were waited for; matrix products, arithmetic and copies ran while one was open for 8% of the time, Pallas kernels for 0%

commit v1 on v0

--- a/solution.py
+++ b/solution.py
@@ -181,7 +181,14 @@
         tiled=True,
     ).astype(jnp.float32)
     incoming = cotangent.astype(jnp.float32)
-    incoming_all = lax.all_gather(cotangent, "tensor", axis=0, tiled=True)
+    ring = [cotangent]
+    for hop in range(3):
+        ring.append(lax.ppermute(ring[-1], "tensor", [(dev, (dev + 1) % 4) for dev in range(4)]))
+    incoming_all = jnp.roll(
+        jnp.concatenate(ring[::-1], axis=0),
+        (lax.axis_index("tensor") + 1) * ring[0].shape[0],
+        axis=0,
+    )
     grad_down = jnp.einsum("tf,td->fd", active, incoming_all, preferred_element_type=jnp.float32)
     grad_active = jnp.einsum(
         "td,fd->tf", incoming_all, full_down, preferred_element_type=jnp.float32

time: 778 us -> 750 us (0.964)
  waiting for transfers between devices: 259 us -> 225 us
    ppermute x0 -> x3, waiting for transfers between devices: none -> 33.7 us  [shards(): lax.ppermute(ring[-1], 'tensor', [(dev, (dev + 1) % 4) for dev in range(4)])]
    all_gather x1, waiting for transfers between devices: 22.3 us -> 0.01 us  [shards(): normed_two_all = lax.all_gather(normed_two, 'tensor', axis=0, tiled=True)]
    all_gather x1 -> x0, waiting for transfers between devices: 21.9 us -> none  [shards(): incoming_all = lax.all_gather(cotangent, 'tensor', axis=0, tiled=True)]
    all_gather x1, waiting for transfers between devices: 38.4 us -> 27.1 us  [shards(): lax.all_gather(w_down, 'dp', axis=1, tiled=True)]
    all_gather x1, waiting for transfers between devices: 8.94 us -> 0.01 us  [shards(): lax.all_gather(w_up, 'dp', axis=0, tiled=True)]
  transfers between devices with their start and end apart: 18 -> 20, of which waited for: 12 -> 12; matrix products, arithmetic and copies ran while one was open for 8% -> 10% of each run, Pallas kernels for 0% -> 0%
where the time goes in v1:
time: 750 us; the launch traced here: 744 us
  waiting for transfers between devices  225 us (30%)
  blocking collectives  169 us (23%)
  matrix products  153 us (20%)
  other arithmetic  104 us (14%)
  local copies, waits for them, and re-layouts  50 us (7%)
  starting transfers between devices  24.5 us (3%)
  between operations  16.8 us (2%)
    all_to_all x4, waiting for transfers between devices, sum_at_owner(): lax.all_to_all(tiles, axis, split_axis=0, concat_axis=0, tiled=True)  50.7 us
    dot_general x4, matrix products, scores_of(): jnp.einsum('qhd,khd->hqk', query_block, key_block, preferred_element_type...  46.2 us
    all_gather x1, blocking collectives, shards(): lax.all_gather(w_out, 'dp', axis=1, tiled=True)  46 us
    ppermute x3, waiting for transfers between devices, shards(): lax.ppermute(ring[-1], 'tensor', [(dev, (dev + 1) % 4) for dev in range(4)])  33.7 us
    reduce_scatter x1, waiting for transfers between devices, shards(): lax.psum_scatter(jnp.dot(context, full_out, preferred_element_type=jnp.fl...  32.7 us
    all_gather x1, blocking collectives, shards(): lax.all_gather(w_key, 'dp', axis=0, tiled=True)  31.2 us
    all_gather x1, blocking collectives, shards(): lax.all_gather(w_value, 'dp', axis=0, tiled=True)  31.2 us
    all_gather x1, blocking collectives, shards(): lax.all_gather(w_query, 'dp', axis=0, tiled=True)  31 us
  transfers between devices with their start and end apart: 20, of which 12 were waited for; matrix products, arithmetic and copies ran while one was open for 10% of the time, Pallas kernels for 0%

profile of v1, /device:TPU:0, one launch (start us, length us, event | category | flops | bytes accessed | tf_op | source)
XLA Modules:
  0.0 744.1 jit_solution(6863624155805615727)
XLA Ops:
  12.9 23.7 %all-reduce.5 = (bf16[768]{0:T(1024)(128)(2,1)S(1)}, bf16[768]{0:T(1024)(128)(2,1)}) all-reduce(bf16[768]{0:T(1024)(128)(2,1)S(1)} %dynamic-update-slice, bf16[768]{0:T(1024)(128)(2,1)S(1)} %dynamic-update-slice.1), channel_id=1, replica_groups=mesh['dp'=8,'tensor'=4] {'dp'}, use_global_device_ids=true, to_apply=%add.2 | all-reduce | flops 1536 | bytes 6144
  41.0 31.2 %all_gather.35 = bf16[768,192]{1,0:T(8,128)(2,1)S(1)} all-gather(bf16[96,192]{1,0:T(8,128)(2,1)} %param.22), channel_id=1, replica_groups=mesh['dp'=8,'tensor'=4] {'dp'}, dimensions={0}, use_global_device_ids=true | all-gather | bytes 331776 | tf_op jit(solution)/shard_map/all_gather | solution.py:78
  72.2 31.2 %all_gather.36 = bf16[768,192]{1,0:T(8,128)(2,1)S(1)} all-gather(bf16[96,192]{1,0:T(8,128)(2,1)} %param.23), channel_id=1, replica_groups=mesh['dp'=8,'tensor'=4] {'dp'}, dimensions={0}, use_global_device_ids=true | all-gather | bytes 331776 | tf_op jit(solution)/shard_map/all_gather | solution.py:79
  110.2 46.0 %all_gather.38 = bf16[192,768]{0,1:T(8,128)(2,1)} all-gather(bf16[192,96]{0,1:T(8,128)(2,1)S(1)} %copy.48), channel_id=1, replica_groups=mesh['dp'=8,'tensor'=4] {'dp'}, dimensions={1}, use_global_device_ids=true | all-gather | bytes 331776 | tf_op jit(solution)/shard_map/all_gather | solution.py:80
  156.2 31.0 %all_gather.37 = bf16[768,192]{1,0:T(8,128)(2,1)S(1)} all-gather(bf16[96,192]{1,0:T(8,128)(2,1)S(1)} %copy-done.35), channel_id=1, replica_groups=mesh['dp'=8,'tensor'=4] {'dp'}, dimensions={0}, use_global_device_ids=true | all-gather | bytes 331776 | tf_op jit(solution)/shard_map/all_gather | solution.py:77
  193.2 72.5 %while.29 = (s32[]{:T(128)}, bf16[2,640,192]{1,2,0:T(8,128)(2,1)}, f32[2,3,640]{2,1,0:T(4,128)S(1)}, s32[2]{0:T(128)S(1)}, bf16[2816,384]{0,1:T(8,128)(2,1)}, /*...) while((s32[]{:T(128)}, bf16[2,640,192]{1,2,0:T(8,128)(2,1)}, ...), condition=%wide.region_6.7_spmd.clone, body=%wide.region_3.6_spmd.clone.sunk | while | flops 1133730560 | bytes 66249560 | solution.py:163
  201.3 8.0 %fusion.144 = (f32[3,640]{1,0:T(4,128)S(1)}, f32[3,640,2176]{2,1,0:T(8,128)}) fusion(pred[640,2176]{1,0:T(8,128)(4,1)S(1)} %fusion.143, bf16[640,3,64]{0,2,1:T(8,128)(2,1)S(1)} %bitcast.144, bf16[2176,3,64]{0,2,1:T(8,128)(2,1)S(1)} %bitcast.143), kind=kOutput, calls=%fused_computation.7.clone.1 | convolution fusion | flops 547305600 | bytes 19193344 | tf_op jit(solution)/shard_map/while/body/eval_jaxpr/qhd,khd->hqk/dot_general | solution.py:146
  209.3 10.5 %fusion.145 = f32[3,640]{1,0:T(4,128)S(1)} fusion(f32[3,640,2176]{2,1,0:T(8,128)} %get-tuple-element.567, f32[3,640]{1,0:T(4,128)S(1)} %get-tuple-element.568, pred[640,2176]{1,0:T(8,128)(4,1)S(1)} %fusion.143), kind=kLoop, calls=%fused_computation.8.clone.1 | loop fusion | flops 16709760 | bytes 18119680 | tf_op jit(solution)/shard_map/while/body/eval_jaxpr/reduce_sum | solution.py:155
  219.8 8.9 %fusion.146 = bf16[3,64,640]{2,1,0:T(8,128)(2,1)S(1)} fusion(bf16[2176,3,64]{0,2,1:T(8,128)(2,1)S(1)} %bitcast.142, f32[3,640,2176]{2,1,0:T(8,128)} %get-tuple-element.567, f32[3,640]{1,0:T(4,128)S(1)} %fusion.145, f32[3,640]{1,0:T(4,128)S(1)} %get-tuple-element.568, pred[640,2176]{1,0:T(8,128)(4,1)S(1)} %fusion.143), kind=kOutput, calls=%fused_computation.15.clone.1 | convolution fusion | flops 555786240 | bytes 19201024 | tf_op jit(solution)/shard_map/while/body/eval_jaxpr/hqk,khd->qhd/dot_general | solution.py:157
  237.5 8.0 %fusion.144 = (f32[3,640]{1,0:T(4,128)S(1)}, f32[3,640,2176]{2,1,0:T(8,128)}) fusion(pred[640,2176]{1,0:T(8,128)(4,1)S(1)} %fusion.143, bf16[640,3,64]{0,2,1:T(8,128)(2,1)S(1)} %bitcast.144, bf16[2176,3,64]{0,2,1:T(8,128)(2,1)S(1)} %bitcast.143), kind=kOutput, calls=%fused_computation.7.clone.1 | convolution fusion | flops 547305600 | bytes 19193344 | tf_op jit(solution)/shard_map/while/body/eval_jaxpr/qhd,khd->hqk/dot_general | solution.py:146
  245.5 10.5 %fusion.145 = f32[3,640]{1,0:T(4,128)S(1)} fusion(f32[3,640,2176]{2,1,0:T(8,128)} %get-tuple-element.567, f32[3,640]{1,0:T(4,128)S(1)} %get-tuple-element.568, pred[640,2176]{1,0:T(8,128)(4,1)S(1)} %fusion.143), kind=kLoop, calls=%fused_computation.8.clone.1 | loop fusion | flops 16709760 | bytes 18119680 | tf_op jit(solution)/shard_map/while/body/eval_jaxpr/reduce_sum | solution.py:155
  256.0 8.8 %fusion.146 = bf16[3,64,640]{2,1,0:T(8,128)(2,1)S(1)} fusion(bf16[2176,3,64]{0,2,1:T(8,128)(2,1)S(1)} %bitcast.142, f32[3,640,2176]{2,1,0:T(8,128)} %get-tuple-element.567, f32[3,640]{1,0:T(4,128)S(1)} %fusion.145, f32[3,640]{1,0:T(4,128)S(1)} %get-tuple-element.568, pred[640,2176]{1,0:T(8,128)(4,1)S(1)} %fusion.143), kind=kOutput, calls=%fused_computation.15.clone.1 | convolution fusion | flops 555786240 | bytes 19201024 | tf_op jit(solution)/shard_map/while/body/eval_jaxpr/hqk,khd->qhd/dot_general | solution.py:157
  271.0 32.7 %reduce-scatter.5.cloned.1.call-done = bf16[320,768]{1,0:T(8,128)(2,1)} async-done(((bf16[1280,768]{1,0:T(8,128)(2,1)}), bf16[320,768]{1,0:T(8,128)(2,1)}) %reduce-scatter.5.cloned.1.call-update) | async-done | bytes 491536 | tf_op jit(solution)/shard_map/reduce_scatter | solution.py:165
  307.2 8.2 %collective-permute-done.2 = bf16[320,768]{1,0:T(8,128)(2,1)S(1)} collective-permute-done((bf16[320,768]{1,0:T(8,128)(2,1)S(1)}, bf16[320,768]{1,0:T(8,128)(2,1)S(1)}, u32[]{:S(2)}, u32[]{:S(2)}) %collective-permute-start.2) | collective-permute-done | bytes 491552 | tf_op jit(solution)/shard_map/ppermute | solution.py:186
  315.4 8.3 %collective-permute-done.3 = bf16[320,768]{1,0:T(8,128)(2,1)S(1)} collective-permute-done((bf16[320,768]{1,0:T(8,128)(2,1)S(1)}, bf16[320,768]{1,0:T(8,128)(2,1)S(1)}, u32[]{:S(2)}, u32[]{:S(2)}) %collective-permute-start.3) | collective-permute-done | bytes 491552 | tf_op jit(solution)/shard_map/ppermute | solution.py:186
  323.8 17.2 %collective-permute-done.4 = bf16[320,768]{1,0:T(8,128)(2,1)S(1)} collective-permute-done((bf16[320,768]{1,0:T(8,128)(2,1)S(1)}, bf16[320,768]{1,0:T(8,128)(2,1)S(1)}, u32[]{:S(2)}, u32[]{:S(2)}) %collective-permute-start.4) | collective-permute-done | bytes 491552 | tf_op jit(solution)/shard_map/ppermute | solution.py:186
  347.6 13.2 %multiply_convert_fusion.1 = (bf16[1280,768]{1,0:T(8,128)(2,1)}, f32[1280,768]{1,0:T(8,128)}, f32[1280,768]{1,0:T(8,128)}) fusion(bf16[1280,768]{1,0:T(8,128)(2,1)} %all-gather.8.cloned.1.call-done, bf16[768,768]{1,0:T(8,128)(2,1)} %all-gather.10.cloned.1.call-done), kind=kOutput, calls=%fused_computation.48 | convolution fusion | flops 1573847040 | bytes 12976128 | tf_op jit(solution)/shard_map/dot_general | solution.py:175
  360.7 27.1 %all-gather.12.cloned.1.call-done = bf16[768,768]{0,1:T(8,128)(2,1)} async-done(((bf16[768,96]{0,1:T(8,128)(2,1)}), bf16[768,768]{0,1:T(8,128)(2,1)}) %all-gather.12.cloned.1.call-update) | async-done | bytes 1179664 | tf_op jit(solution)/shard_map/all_gather | solution.py:83
  387.8 7.1 add_convert_fusion
  399.3 29.2 %reduce-scatter.9.cloned.1.call-done = bf16[320,768]{1,0:T(8,128)(2,1)} async-done(((bf16[1280,768]{1,0:T(8,128)(2,1)}), bf16[320,768]{1,0:T(8,128)(2,1)}) %reduce-scatter.9.cloned.1.call-update) | async-done | bytes 491536 | tf_op jit(solution)/shard_map/reduce_scatter | solution.py:201
  433.4 21.4 %all-gather.14.cloned.1.call-done = bf16[1280,768]{1,0:T(8,128)(2,1)} async-done(((bf16[320,768]{1,0:T(8,128)(2,1)}), bf16[1280,768]{1,0:T(8,128)(2,1)}) %all-gather.14.cloned.1.call-update) | async-done | bytes 1966096 | tf_op jit(solution)/shard_map/all_gather | solution.py:211
  461.0 112.5 %while.30 = (s32[]{:T(128)}, bf16[1280,192]{0,1:T(8,128)(2,1)}, f32[2816,384]{0,1:T(8,128)}, bf16[2816,384]{0,1:T(8,128)(2,1)}, s32[2816]{0:T(1024)S(1)}, /*inde...) while((s32[]{:T(128)}, bf16[1280,192]{0,1:T(8,128)(2,1)}, ...), condition=%wide.region_14.15_spmd.clone, body=%wide.region_12.14_spmd.clone.sunk | while | flops 2727729920 | bytes 220916592 | solution.py:260
  468.7 8.1 %fusion.158 = f32[3,640,2176]{2,1,0:T(8,128)} fusion(bf16[640,3,64]{0,2,1:T(8,128)(2,1)S(1)} %bitcast.139, bf16[2176,3,64]{0,2,1:T(8,128)(2,1)S(1)} %bitcast.138), kind=kOutput, calls=%fused_computation.152.clone.1 | convolution fusion | flops 534773760 | bytes 17793024 | tf_op jit(solution)/shard_map/while/body/eval_jaxpr/qhd,khd->hqk/dot_general | solution.py:226
  476.8 15.1 %multiply_reduce_fusion.3 = (f32[3,640]{1,0:T(4,128)S(1)}, f32[3,640,2176]{2,1,0:T(8,128)}) fusion(f32[3,640,2176]{2,1,0:T(8,128)} %fusion.158, f32[3,640]{1,0:T(4,128)S(1)} %dynamic-slice_bitcast_fusion.2, bf16[640,3,64]{0,2,1:T(8,128)(2,1)S(1)} %bitcast.136, bf16[2176,3,64]{0,2,1:T(8,128)(2,1)S(1)} %bitcast.133, pred[640,2176]{1,0:T(8,128)(4,1)S(1)} %fusion.159), kind=kOutput, calls=%fused_computation.24.clone.1 | convolution fusion | flops 555661440 | bytes 35912704 | tf_op jit(solution)/shard_map/while/body/eval_jaxpr/qhd,khd->hqk/dot_general | solution.py:146
  491.9 11.4 %multiply_convert_fusion.4 = bf16[3,640,2176]{2,1,0:T(8,128)(2,1)S(1)} fusion(f32[3,640,2176]{2,1,0:T(8,128)} %get-tuple-element.584, f32[3,640,2176]{2,1,0:T(8,128)} %fusion.158, f32[3,640]{1,0:T(4,128)S(1)} %get-tuple-element.585), kind=kLoop, calls=%fused_computation.23.clone.1 | loop fusion | flops 12533760 | bytes 41786880 | tf_op jit(solution)/shard_map/while/body/eval_jaxpr/convert_element_type | solution.py:230
  525.0 8.1 %fusion.158 = f32[3,640,2176]{2,1,0:T(8,128)} fusion(bf16[640,3,64]{0,2,1:T(8,128)(2,1)S(1)} %bitcast.139, bf16[2176,3,64]{0,2,1:T(8,128)(2,1)S(1)} %bitcast.138), kind=kOutput, calls=%fused_computation.152.clone.1 | convolution fusion | flops 534773760 | bytes 17793024 | tf_op jit(solution)/shard_map/while/body/eval_jaxpr/qhd,khd->hqk/dot_general | solution.py:226
  533.1 15.1 %multiply_reduce_fusion.3 = (f32[3,640]{1,0:T(4,128)S(1)}, f32[3,640,2176]{2,1,0:T(8,128)}) fusion(f32[3,640,2176]{2,1,0:T(8,128)} %fusion.158, f32[3,640]{1,0:T(4,128)S(1)} %dynamic-slice_bitcast_fusion.2, bf16[640,3,64]{0,2,1:T(8,128)(2,1)S(1)} %bitcast.136, bf16[2176,3,64]{0,2,1:T(8,128)(2,1)S(1)} %bitcast.133, pred[640,2176]{1,0:T(8,128)(4,1)S(1)} %fusion.159), kind=kOutput, calls=%fused_computation.24.clone.1 | convolution fusion | flops 555661440 | bytes 35912704 | tf_op jit(solution)/shard_map/while/body/eval_jaxpr/qhd,khd->hqk/dot_general | solution.py:146
  548.2 11.4 %multiply_convert_fusion.4 = bf16[3,640,2176]{2,1,0:T(8,128)(2,1)S(1)} fusion(f32[3,640,2176]{2,1,0:T(8,128)} %get-tuple-element.584, f32[3,640,2176]{2,1,0:T(8,128)} %fusion.158, f32[3,640]{1,0:T(4,128)S(1)} %get-tuple-element.585), kind=kLoop, calls=%fused_computation.23.clone.1 | loop fusion | flops 12533760 | bytes 41786880 | tf_op jit(solution)/shard_map/while/body/eval_jaxpr/convert_element_type | solution.py:230
  579.7 27.4 %collective-permute-done.6 = bf16[256,384]{0,1:T(8,128)(2,1)S(1)} collective-permute-done((bf16[256,384]{0,1:T(8,128)(2,1)S(1)}, bf16[256,384]{0,1:T(8,128)(2,1)S(1)}, u32[]{:S(2)}, u32[]{:S(2)}) %collective-permute-start.6) | collective-permute-done | bytes 196640 | tf_op jit(solution)/shard_map/ppermute | solution.py:16
  639.3 10.7 %all-to-all-done.3 = bf16[8,768,96]{1,2,0:T(8,128)(2,1)} async-done(((bf16[8,768,96]{1,2,0:T(8,128)(2,1)}), bf16[8,768,96]{1,2,0:T(8,128)(2,1)}, u32[]{:S(2)}, u32[]{:S(2)}) %all-to-all-start.3) | async-done | bytes 1179680 | tf_op jit(solution)/shard_map/all_to_all | solution.py:27
  682.0 15.7 %all-to-all-done = bf16[8,96,577]{2,1,0:T(8,128)(2,1)S(1)} async-done(((bf16[8,96,577]{2,1,0:T(8,128)(2,1)}), bf16[8,96,577]{2,1,0:T(8,128)(2,1)S(1)}, u32[]{:S(2)}, u32[]{:S(2)}) %all-to-all-start) | async-done | bytes 886304 | tf_op jit(solution)/shard_map/all_to_all | solution.py:27
  710.7 24.3 %all-to-all-done.2 = bf16[8,96,769]{2,1,0:T(8,128)(2,1)S(1)} async-done(((bf16[8,96,769]{2,1,0:T(8,128)(2,1)}), bf16[8,96,769]{2,1,0:T(8,128)(2,1)S(1)}, u32[]{:S(2)}, u32[]{:S(2)}) %all-to-all-start.2) | async-done | bytes 1181216 | tf_op jit(solution)/shard_map/all_to_all | solution.py:27
  (270 shorter events, 196.2 us)
Async XLA Ops:
  8.0 95.4 %all-gather.6.cloned.1.call-start = ((), (), s32[]{:S(2)}) async-start(), calls=%async_computation.8 | async-start | bytes 2457600 | tf_op jit(solution)/shard_map/all_gather | solution.py:101
  9.3 30.9 %copy-start.36 = (f32[320]{0:T(512)}, f32[320]{0:T(512)S(1)}, u32[]{:S(2)}) copy-start(f32[320]{0:T(512)S(1)} %add_rsqrt_fusion.1) | copy-start | bytes 3844
  39.2 264.5 %reduce-scatter.5.cloned.1.call-start = ((), (), s32[]{:S(2)}) async-start(), calls=%async_computation.9 | async-start | bytes 2457600 | tf_op jit(solution)/shard_map/reduce_scatter | solution.py:165
  72.2 36.3 %copy-start.19 = (bf16[768,192]{1,0:T(8,128)(2,1)}, bf16[768,192]{1,0:T(8,128)(2,1)S(1)}, u32[]{:S(2)}) copy-start(bf16[768,192]{1,0:T(8,128)(2,1)S(1)} %all_gather.35) | copy-start | bytes 884740
  103.4 52.9 %copy-start.21 = (bf16[768,192]{1,0:T(8,128)(2,1)}, bf16[768,192]{1,0:T(8,128)(2,1)S(1)}, u32[]{:S(2)}) copy-start(bf16[768,192]{1,0:T(8,128)(2,1)S(1)} %all_gather.36) | copy-start | bytes 884740
  103.4 52.9 %copy-start.35 = (bf16[96,192]{1,0:T(8,128)(2,1)S(1)}, bf16[96,192]{1,0:T(8,128)(2,1)}, u32[]{:S(2)}) copy-start(bf16[96,192]{1,0:T(8,128)(2,1)} %param.21) | copy-start | bytes 110596
  105.9 82.6 %copy-start.3 = (bf16[1280,768]{1,0:T(8,128)(2,1)S(1)}, bf16[1280,768]{1,0:T(8,128)(2,1)}, u32[]{:S(2)}) copy-start(bf16[1280,768]{1,0:T(8,128)(2,1)} %all-gather.6.cloned.1.call-done) | copy-start | bytes 5898244
  108.5 83.2 %collective-permute-start.1 = (bf16[1280,384]{0,1:T(8,128)(2,1)S(1)}, bf16[1280,384]{0,1:T(8,128)(2,1)S(1)}, u32[]{:S(2)}, u32[]{:S(2)}) collective-permute-start(bf16[1280,384]{0,1:T(8,128)(2,1)S(1)} %pad_maximum_fusion.1), channel_id=1, source_target_pairs={{0,4},{4,8},{8,12},{12,16},{16,20},{20,24},{24,28},{1,5},{5,9},{9,... | collective-permute-start | bytes 2949128 | tf_op jit(solution)/shard_map/ppermute | solution.py:16
  187.2 4.5 collective-permute-start
  265.7 38.0 %copy-start.1 = (bf16[320,768]{1,0:T(8,128)(2,1)S(1)}, bf16[320,768]{1,0:T(8,128)(2,1)}, u32[]{:S(2)}) copy-start(bf16[320,768]{1,0:T(8,128)(2,1)} %param.16) | copy-start | bytes 1474564
  266.8 40.2 %copy-start.10 = (bf16[2,24,8,640]{3,2,0,1:T(8,128)(2,1)}, bf16[2,24,8,640]{3,2,0,1:T(8,128)(2,1)S(1)}, u32[]{:S(2)}) copy-start(bf16[2,24,8,640]{3,2,0,1:T(8,128)(2,1)S(1)} %copy.67) | copy-start | bytes 1474564
  266.8 40.3 %copy-start.7 = (bf16[320,768]{1,0:T(8,128)(2,1)S(1)}, bf16[320,768]{1,0:T(8,128)(2,1)}, u32[]{:S(2)}) copy-start(bf16[320,768]{1,0:T(8,128)(2,1)} %param.17) | copy-start | bytes 1474564
  270.1 77.4 %all-gather.10.cloned.1.call-start = ((), (), s32[]{:S(2)}) async-start(), calls=%async_computation.11 | async-start | bytes 1327104 | tf_op jit(solution)/shard_map/all_gather | solution.py:82
  270.7 76.9 %all-gather.8.cloned.1.call-start = ((), (), s32[]{:S(2)}) async-start(), calls=%async_computation.10 | async-start | bytes 2457600 | tf_op jit(solution)/shard_map/all_gather | solution.py:174
  271.0 159.7 %copy-start.29 = (f32[768]{0:T(1024)}, f32[768]{0:T(1024)S(1)}, u32[]{:S(2)}) copy-start(f32[768]{0:T(1024)S(1)} %convert_element_type.159) | copy-start | bytes 9220
  305.0 125.7 %copy-start.33 = (f32[320]{0:T(512)}, f32[320]{0:T(512)S(1)}, u32[]{:S(2)}) copy-start(f32[320]{0:T(512)S(1)} %add_rsqrt_fusion) | copy-start | bytes 3844
  307.1 80.7 %all-gather.12.cloned.1.call-start = ((), (), s32[]{:S(2)}) async-start(), calls=%async_computation.12 | async-start | bytes 1327104 | tf_op jit(solution)/shard_map/all_gather | solution.py:83
  307.1 8.3 %collective-permute-start.2 = (bf16[320,768]{1,0:T(8,128)(2,1)S(1)}, bf16[320,768]{1,0:T(8,128)(2,1)S(1)}, u32[]{:S(2)}, u32[]{:S(2)}) collective-permute-start(bf16[320,768]{1,0:T(8,128)(2,1)S(1)} %copy-done.7), channel_id=1, source_target_pairs={{0,1},{1,2},{2,3},{3,0},{4,5},{5,6},{6,7},{7,4},{8,9},{9,10},{10,1... | collective-permute-start | bytes 1474568 | tf_op jit(solution)/shard_map/ppermute | solution.py:186
  315.4 8.3 %collective-permute-start.3 = (bf16[320,768]{1,0:T(8,128)(2,1)S(1)}, bf16[320,768]{1,0:T(8,128)(2,1)S(1)}, u32[]{:S(2)}, u32[]{:S(2)}) collective-permute-start(bf16[320,768]{1,0:T(8,128)(2,1)S(1)} %collective-permute-done.2), channel_id=1, source_target_pairs={{0,1},{1,2},{2,3},{3,0},{4,5},{5,6},{6,7},{7,4},{8,9},{9,10},{10,1... | collective-permute-start | bytes 1474568 | tf_op jit(solution)/shard_map/ppermute | solution.py:186
  323.7 17.3 %collective-permute-start.4 = (bf16[320,768]{1,0:T(8,128)(2,1)S(1)}, bf16[320,768]{1,0:T(8,128)(2,1)S(1)}, u32[]{:S(2)}, u32[]{:S(2)}) collective-permute-start(bf16[320,768]{1,0:T(8,128)(2,1)S(1)} %collective-permute-done.3), channel_id=1, source_target_pairs={{0,1},{1,2},{2,3},{3,0},{4,5},{5,6},{6,7},{7,4},{8,9},{9,10},{10,1... | collective-permute-start | bytes 1474568 | tf_op jit(solution)/shard_map/ppermute | solution.py:186
  323.7 104.8 %reduce-scatter.9.cloned.1.call-start = ((), (), s32[]{:S(2)}) async-start(), calls=%async_computation.14 | async-start | bytes 2457600 | tf_op jit(solution)/shard_map/reduce_scatter | solution.py:201
  396.2 32.3 %copy-start.5 = (bf16[320,768]{1,0:T(8,128)(2,1)S(1)}, bf16[320,768]{1,0:T(8,128)(2,1)}, u32[]{:S(2)}) copy-start(bf16[320,768]{1,0:T(8,128)(2,1)} %reduce-scatter.5.cloned.1.call-done) | copy-start | bytes 1474564
  399.2 55.5 %copy-start.25 = (bf16[192,768]{0,1:T(8,128)(2,1)S(1)}, bf16[192,768]{0,1:T(8,128)(2,1)}, u32[]{:S(2)}) copy-start(bf16[192,768]{0,1:T(8,128)(2,1)} %all_gather.38) | copy-start | bytes 884740
  399.3 55.5 %all-gather.14.cloned.1.call-start = ((), (), s32[]{:S(2)}) async-start(), calls=%async_computation.15 | async-start | bytes 2457600 | tf_op jit(solution)/shard_map/all_gather | solution.py:211
  432.9 223.7 %reduce-scatter.11.cloned.1.call-start = ((), (), s32[]{:S(2)}) async-start(), calls=%async_computation.16 | async-start | bytes 2457600 | tf_op jit(solution)/shard_map/reduce_scatter | solution.py:285
  576.2 30.9 %collective-permute-start.5 = (bf16[1280,384]{0,1:T(8,128)(2,1)S(1)}, bf16[1280,384]{0,1:T(8,128)(2,1)S(1)}, u32[]{:S(2)}, u32[]{:S(2)}) collective-permute-start(bf16[1280,384]{0,1:T(8,128)(2,1)S(1)} %slice.58), channel_id=1, source_target_pairs={{4,0},{8,4},{12,8},{16,12},{20,16},{24,20},{28,24},{5,1},{9,5},{13... | collective-permute-start | bytes 2949128 | tf_op jit(solution)/shard_map/ppermute | solution.py:16
  577.7 29.4 %collective-permute-start.6 = (bf16[256,384]{0,1:T(8,128)(2,1)S(1)}, bf16[256,384]{0,1:T(8,128)(2,1)S(1)}, u32[]{:S(2)}, u32[]{:S(2)}) collective-permute-start(bf16[256,384]{0,1:T(8,128)(2,1)S(1)} %slice.59), channel_id=1, source_target_pairs={{8,0},{12,4},{16,8},{20,12},{24,16},{28,20},{9,1},{13,5},{17,9},{2... | collective-permute-start | bytes 589832 | tf_op jit(solution)/shard_map/ppermute | solution.py:16
  617.4 32.7 %all-to-all-start.3 = ((bf16[8,768,96]{1,2,0:T(8,128)(2,1)}), bf16[8,768,96]{1,2,0:T(8,128)(2,1)}, u32[]{:S(2)}, u32[]{:S(2)}) async-start(bf16[8,768,96]{1,2,0:T(8,128)(2,1)} %bitcast.8), calls=%async_computation.7 | async-start | bytes 2359296 | tf_op jit(solution)/shard_map/all_to_all | solution.py:27
  621.6 84.5 %reduce-scatter.7.cloned.1.call-start = ((), (), s32[]{:S(2)}) async-start(), calls=%async_computation.13 | async-start | bytes 2457600 | tf_op jit(solution)/shard_map/reduce_scatter | solution.py:177
  650.1 17.4 %all-to-all-start.1 = ((bf16[8,192,96]{2,1,0:T(8,128)(2,1)}), bf16[8,192,96]{2,1,0:T(8,128)(2,1)}, u32[]{:S(2)}, u32[]{:S(2)}) async-start(bf16[8,192,96]{2,1,0:T(8,128)(2,1)} %bitcast.148), calls=%async_computation.5 | async-start | bytes 786432 | tf_op jit(solution)/shard_map/all_to_all | solution.py:27
  667.5 30.2 %all-to-all-start = ((bf16[8,96,577]{2,1,0:T(8,128)(2,1)}), bf16[8,96,577]{2,1,0:T(8,128)(2,1)S(1)}, u32[]{:S(2)}, u32[]{:S(2)}) async-start(bf16[8,96,577]{2,1,0:T(8,128)(2,1)} %pad_maximum_fusion.2), calls=%async_computation.4 | async-start | bytes 1966080 | tf_op jit(solution)/shard_map/all_to_all | solution.py:27
  698.7 36.4 %all-to-all-start.2 = ((bf16[8,96,769]{2,1,0:T(8,128)(2,1)}), bf16[8,96,769]{2,1,0:T(8,128)(2,1)S(1)}, u32[]{:S(2)}, u32[]{:S(2)}) async-start(bf16[8,96,769]{2,1,0:T(8,128)(2,1)} %pad_maximum_fusion), calls=%async_computation.6 | async-start | bytes 2752512 | tf_op jit(solution)/shard_map/all_to_all | solution.py:27
  (39 other events, 467.9 us)
Sparse Core Ops, SparseCore 0:
  39.3 19.0 all-gather.5
  270.2 33.4 reduce-scatter.4
  399.4 29.0 reduce-scatter.8
Sparse Core Ops, SparseCore 1:
  272.8 44.3 all-gather.9
  319.2 24.7 all-gather.7
  346.3 41.5 all-gather.11
  433.0 21.7 all-gather.13
  612.4 28.7 reduce-scatter.10
  643.9 30.6 reduce-scatter.6
